TPU v7x, 32 devices: a whole 2x2x4 slice. The times are simulated.
32 devices in a mesh: groups: 2 (over y), gx: 4 (over z), gy: 2 (over x), gz: 2 (over core).
Axes of the slice: x: 2, y: 2, z: 4, core: 2. Of those that a mesh axis runs over, the one named last changes fastest.
Arguments:
- tokens: bfloat16 [192, 8192], P(('groups', 'gx', 'gy'), 'gz'), parts along dimension 0, may hold values from -6 to 6
- gate_weight: bfloat16 [8192, 14336], P('gz', ('gx', 'gy')), may hold values from -0.0625 to 0.0625
- up_weight: bfloat16 [8192, 14336], P('gz', ('gx', 'gy')), may hold values from -0.0625 to 0.0625
- down_weight: bfloat16 [14336, 8192], P('gx', ('gy', 'gz')), may hold values from -0.046875 to 0.046875
- reward_weight: bfloat16 [8192], P(('gy', 'gz')), may hold values from -0.0625 to 0.0625
- candidate_ids: int32 [192], P('groups'), parts along dimension 0, may hold values from 0 to 15, never falling along the last dimension, each value on 1 to 12 neighbouring positions
Outputs:
- mixed: bfloat16 [192, 8192], P(('groups', 'gx'), ('gy', 'gz')), parts along dimension 0
- scores: float32 [32], P('groups'), parts along dimension 0
There are 2 independent parts, one for each index of `groups`. A program takes and returns all parts, laid end to end along the dimension named above; an argument that names none is the same for every part. Nothing has to cross between parts.
Inputs may be any that keep to these rules, and one draw needn't show every extreme that they name: `candidate_ids`: numbers never fall along the tokens; every candidate has 1 to 12 consecutive tokens, one exactly 12.
All inputs are finite; a program needn't handle non-finite values.
Results may differ from a plain program's by a relative error of at most 0.03.
Values may be sent and summed in bfloat16 or wider, within the bound.
A program may use at most 128 MiB of HBM per device.

v0:
```python
import jax
import jax.numpy as jnp
from jax import lax
from jax.sharding import PartitionSpec as P

CANDS = 16


def swiglu_pair(summed, unit_count):
    row_count = summed.shape[0]
    split_pair = summed.reshape(row_count, -1, 2, unit_count)
    gate_part = split_pair[:, :, 0, :].reshape(row_count, -1)
    upper_part = split_pair[:, :, 1, :].reshape(row_count, -1)
    return (jax.nn.silu(gate_part) * upper_part).astype(jnp.bfloat16)


def combine_pairs(partial_value, unit_count):
    summed = lax.psum(partial_value.astype(jnp.bfloat16), "gz").astype(jnp.float32)
    return swiglu_pair(summed, unit_count)


def local(tokens, gate_weight, up_weight, down_weight, reward_weight, candidate_ids):
    unit_count = gate_weight.shape[1]
    paired = jnp.concatenate([gate_weight, up_weight], axis=1)
    local_rows = tokens.shape[0]
    gy_count = lax.axis_size("gy")
    out_rows = local_rows * gy_count
    all_tokens = lax.all_gather(tokens, ("gx", "gy"), axis=0, tiled=True)
    partial_value = jnp.dot(all_tokens, paired, preferred_element_type=jnp.float32)
    hidden_part = combine_pairs(partial_value, unit_count)
    hidden_all = lax.all_gather(hidden_part, "gy", axis=1, tiled=True)
    summed_out = lax.psum_scatter(
        jnp.dot(hidden_all, down_weight, preferred_element_type=jnp.float32).astype(jnp.bfloat16),
        "gx",
        scatter_dimension=0,
        tiled=True,
    )
    values = jnp.dot(summed_out, reward_weight, preferred_element_type=jnp.float32)
    first_row = lax.axis_index("gx") * out_rows
    extended = jnp.concatenate([candidate_ids, jnp.full((1,), -1, jnp.int32)])
    own_ids = lax.dynamic_slice_in_dim(extended, first_row, out_rows, 0)
    next_ids = lax.dynamic_slice_in_dim(extended, first_row + 1, out_rows, 0)
    matches = (own_ids[:, None] == jnp.arange(CANDS, dtype=jnp.int32)[None, :]) & (
        own_ids != next_ids
    )[:, None]
    partial_scores = jnp.sum(
        jnp.where(matches, values[:, None], jnp.zeros_like(values)[:, None]), axis=0
    )
    scores = lax.psum(partial_scores, ("gx", "gy", "gz"))
    return (summed_out, scores)


def solution(mesh):
    placed = (
        P(("groups", "gx", "gy"), "gz"),
        P("gz", ("gx", "gy")),
        P("gz", ("gx", "gy")),
        P("gx", ("gy", "gz")),
        P(("gy", "gz")),
        P("groups"),
    )
    return jax.shard_map(
        local,
        mesh=mesh,
        in_specs=placed,
        out_specs=(P(("groups", "gx"), ("gy", "gz")), P("groups")),
        check_vma=False,
    )
```

profile of v0, /device:TPU:0, one launch (start us, length us, event | category | flops | bytes accessed | tf_op | source)
XLA Modules:
  0.0 156.6 jit_solution(13745215039404218617)
XLA Ops:
  7.2 0.0 all-reduce.2.cloned.1.call-start
  7.2 34.9 %all-gather = bf16[8,12,4096]{2,1,0:T(8,128)(2,1)S(1)} all-gather(bf16[1,12,4096]{2,1,0:T(8,128)(2,1)} %bitcast.18), channel_id=1, replica_groups=mesh['groups'=2,'gx'=4,'gy'=2,'gz'=2] {'gx','gy'}, dimensions={0}, use_global_device_ids=true | all-gather | bytes 884736 | tf_op jit(solution)/shard_map/all_gather | solution.py:28
  42.1 0.2 reshape.16
  42.3 11.3 %fusion.7 = bf16[96,3584]{1,0:T(8,128)(2,1)S(1)} fusion(bf16[96,4096]{1,0:T(8,128)(2,1)S(1)} %reshape.16, bf16[4096,1792]{1,0:T(8,128)(2,1)} %param.8, bf16[4096,1792]{1,0:T(8,128)(2,1)} %param.7), kind=kOutput, calls=%fused_computation.5 | convolution fusion | flops 2877636608 | bytes 30834688 | tf_op jit(solution)/shard_map/dot_general | solution.py:29
  53.6 1.0 reshape.13
  54.6 0.0 copy-start
  54.6 0.0 copy-start.1
  54.6 0.0 all-reduce.2.cloned.1.call-update
  54.6 0.0 reduce-scatter.2.cloned.1.call-start
  54.6 19.9 %all-reduce.2.cloned.1.call-done = bf16[96,1,2,1792]{3,2,0,1:T(2,128)(2,1)} async-done(((bf16[96,1,2,1792]{3,2,0,1:T(2,128)(2,1)}), bf16[96,1,2,1792]{3,2,0,1:T(2,128)(2,1)}) %all-reduce.2.cloned.1.call-update) | async-done | bytes 688144 | tf_op jit(solution)/shard_map/psum | solution.py:18
  74.6 2.5 %fusion.13 = (f32[96,1,1,1792]{3,2,0,1:T(1,128)S(1)}, f32[96,1,1,1792]{3,2,0,1:T(1,128)S(1)}) fusion(bf16[96,1,2,1792]{3,2,0,1:T(2,128)(2,1)} %all-reduce.2.cloned.1.call-done), kind=kLoop, calls=%fused_computation.17 | loop fusion | bytes 2752512 | tf_op jit(solution)/shard_map/slice | solution.py:12
  77.1 0.2 fusion.10
  77.3 10.9 %all_gather.7 = bf16[96,3584]{1,0:T(8,128)(2,1)S(1)} all-gather(bf16[96,1792]{1,0:T(8,128)(2,1)S(1)} %fusion.10), channel_id=1, replica_groups=mesh['groups'=2,'gx'=4,'gy'=2,'gz'=2] {'gy'}, dimensions={1}, use_global_device_ids=true | all-gather | bytes 1032192 | tf_op jit(solution)/shard_map/all_gather | solution.py:31
  88.2 8.5 %convolution_convert_fusion = bf16[96,2048]{1,0:T(8,128)(2,1)} fusion(bf16[96,3584]{1,0:T(8,128)(2,1)S(1)} %all_gather.7, bf16[3584,2048]{1,0:T(8,128)(2,1)} %param.9), kind=kOutput, calls=%fused_computation.6 | convolution fusion | flops 1409482752 | bytes 15761408 | tf_op jit(solution)/shard_map/dot_general | solution.py:33
  96.7 0.0 reduce-scatter.2.cloned.1.call-update
  96.7 0.0 copy-done
  96.8 0.0 copy-done.1
  96.8 0.1 pad_add_fusion
  96.9 0.1 dynamic-slice_compare_fusion
  96.9 21.7 %reduce-scatter.2.cloned.1.call-done = bf16[24,2048]{1,0:T(8,128)(2,1)} async-done(((bf16[96,2048]{1,0:T(8,128)(2,1)}), bf16[24,2048]{1,0:T(8,128)(2,1)}) %reduce-scatter.2.cloned.1.call-update) | async-done | bytes 98320 | tf_op jit(solution)/shard_map/reduce_scatter | solution.py:32
  118.7 1.0 convolution_bitcast_fusion
  119.7 0.1 select_reduce_fusion
  119.8 30.0 %psum.15 = f32[16]{0:T(128)} all-reduce(f32[16]{0:T(128)S(1)} %select_reduce_fusion), channel_id=1, replica_groups=mesh['groups'=2,'gx'=4,'gy'=2,'gz'=2] {'gx','gy','gz'}, use_global_device_ids=true, to_apply=%region_3.4 | all-reduce | flops 16 | bytes 128 | tf_op jit(solution)/shard_map/psum | solution.py:49
  (1 shorter events, 0.0 us)
Async XLA Ops:
  7.2 67.4 %all-reduce.2.cloned.1.call-start = ((), (), s32[]{:S(2)}) async-start(), calls=%async_computation.1 | async-start | bytes 1376256 | tf_op jit(solution)/shard_map/psum | solution.py:18
  54.6 42.2 %copy-start = (bf16[2048]{0:T(1024)(128)(2,1)S(1)}, bf16[2048]{0:T(1024)(128)(2,1)}, u32[]{:S(2)}) copy-start(bf16[2048]{0:T(1024)(128)(2,1)} %param.10) | copy-start | bytes 12292
  54.6 42.2 %copy-start.1 = (s32[96]{0:T(128)S(1)}, s32[96]{0:T(128)}, u32[]{:S(2)}) copy-start(s32[96]{0:T(128)} %param.11) | copy-start | bytes 1156
  54.6 64.1 %reduce-scatter.2.cloned.1.call-start = ((), (), s32[]{:S(2)}) async-start(), calls=%async_computation.2 | async-start | bytes 491520 | tf_op jit(solution)/shard_map/reduce_scatter | solution.py:32
Sparse Core Ops, SparseCore 0:
  54.7 19.8 all-reduce.1
  96.9 21.7 reduce-scatter.1
where the time goes:
time: 157 us
  blocking collectives  75.8 us (48%)
  waiting for transfers between devices  41.7 us (27%)
  matrix products  20.8 us (13%)
  between operations  14.1 us (9%)
  local copies, waits for them, and re-layouts  3.69 us (2%)
    all_gather x1, blocking collectives, local(): all_tokens = lax.all_gather(tokens, ('gx', 'gy'), axis=0, tiled=True)  34.9 us
    psum x1, blocking collectives, local(): scores = lax.psum(partial_scores, ('gx', 'gy', 'gz'))  30 us
    reduce_scatter x1, waiting for transfers between devices, local(): lax.psum_scatter(jnp.dot(hidden_all, down_weight, preferred_element_type=...  21.7 us
    psum x1, waiting for transfers between devices, combine_pairs(): lax.psum(partial_value.astype(jnp.bfloat16), 'gz').astype(jnp.float32)  19.9 us
    dot_general x1, matrix products, local(): jnp.dot(all_tokens, paired, preferred_element_type=jnp.float32)  11.3 us
    all_gather x1, blocking collectives, local(): hidden_all = lax.all_gather(hidden_part, 'gy', axis=1, tiled=True)  10.9 us
    dot_general x1, matrix products, local(): jnp.dot(hidden_all, down_weight, preferred_element_type=jnp.float32)  8.51 us
  transfers between devices with their start and end apart: 2, of which 2 were waited for; matrix products, arithmetic and copies ran while one was open for 0% of the time, Pallas kernels for 0%

commit v1 on v0

--- a/solution.py
+++ b/solution.py
@@ -1,6 +1,8 @@
 import jax
 import jax.numpy as jnp
 from jax import lax
+from jax.experimental import pallas as pl
+from jax.experimental.pallas import tpu as pltpu
 from jax.sharding import PartitionSpec as P
 
 CANDS = 16
@@ -19,7 +21,7 @@
     return swiglu_pair(summed, unit_count)
 
 
-def local(tokens, gate_weight, up_weight, down_weight, reward_weight, candidate_ids):
+def plain_local(tokens, gate_weight, up_weight, down_weight, reward_weight, candidate_ids):
     unit_count = gate_weight.shape[1]
     paired = jnp.concatenate([gate_weight, up_weight], axis=1)
     local_rows = tokens.shape[0]
@@ -50,7 +52,308 @@
     return (summed_out, scores)
 
 
+MESH = pl.DeviceIdType.MESH
+WIDE = 256
+OUT_WIDE = 512
+VMEM_BYTES = 60 * 1024 * 1024
+
+
+def fused_kernel(
+    sizes, tok_ref, gate_ref, up_ref, down_ref, reward_ref, ids_ref, out_ref, score_ref,
+    tok_f32, x_f32, x_bf, blocks, gate_buf, up_buf, down_buf, part, part_in, hid, term, term_in, score_buf,
+    gate_sem, up_sem, down_sem, tok_send, tok_recv, part_send, part_recv, hid_send, hid_recv,
+    term_send, term_recv, score_send, score_recv,
+):
+    nx, rows, pieces, chunks, out_chunks = sizes
+    cut = tok_ref.shape[1] // pieces
+    out_rows = 2 * rows
+    total_rows = x_bf.shape[0]
+    half = WIDE // 2
+    out_half = OUT_WIDE // 2
+    group, gx, gy, gz = (lax.axis_index(a) for a in ("groups", "gx", "gy", "gz"))
+    gy_other, gz_other = 1 - gy, 1 - gz
+    devices = nx * 4
+    own = (gx * 2 + gy) * 2 + gz
+
+    def peer(step):
+        index = lax.rem(own + step, devices)
+        return (group, index // 4, lax.rem(index // 2, 2), lax.rem(index, 2))
+
+    def weight_copy(source, target, sem, c, width):
+        return pltpu.make_async_copy(
+            source.at[:, pl.ds(pl.multiple_of(c * width, width), width)], target.at[c], sem.at[c]
+        )
+
+    @pl.loop(0, chunks)
+    def _(c):
+        weight_copy(gate_ref, gate_buf, gate_sem, c, WIDE).start()
+        weight_copy(up_ref, up_buf, up_sem, c, WIDE).start()
+
+    @pl.loop(0, out_chunks)
+    def _(c):
+        weight_copy(down_ref, down_buf, down_sem, c, OUT_WIDE).start()
+
+    barrier = pltpu.get_barrier_semaphore()
+
+    @pl.loop(1, devices)
+    def _(step):
+        pl.semaphore_signal(barrier, inc=1, device_id=peer(step), device_id_type=MESH)
+
+    mine = gx * 2 + gy
+    for p in range(pieces):
+        tok_f32[pl.ds(p * rows, rows), :] = tok_ref[:, pl.ds(p * cut, cut)].astype(jnp.float32)
+    blocks[mine] = tok_f32[...].astype(jnp.bfloat16)
+    pl.semaphore_wait(barrier, devices - 1)
+
+    def tok_copy(slot, send, target):
+        return pltpu.make_async_remote_copy(
+            src_ref=blocks.at[slot], dst_ref=blocks.at[slot], send_sem=tok_send.at[send],
+            recv_sem=tok_recv.at[slot], device_id=target, device_id_type=MESH,
+        )
+
+    @pl.loop(1, nx)
+    def _(step):
+        tok_copy(mine, step, (group, lax.rem(gx + step, nx), gy, gz)).start()
+
+    x_peer = (group, gx, gy_other, gz)
+    tok_copy(mine, 0, x_peer).start()
+
+    @pl.loop(1, nx)
+    def _(step):
+        slot = lax.rem(gx + nx - step, nx) * 2 + gy
+        tok_copy(slot, 0, x_peer).wait_recv()
+        tok_copy(slot, nx + step, x_peer).start()
+
+    @pl.loop(0, nx)
+    def _(step):
+        slot = lax.rem(gx + nx - step, nx) * 2 + gy_other
+        tok_copy(slot, 0, x_peer).wait_recv()
+
+    for d in range(nx * 2):
+        tok_f32[...] = blocks[d].astype(jnp.float32)
+        for p in range(pieces):
+            x_f32[pl.ds(d * rows, rows), pl.ds(p * cut, cut)] = tok_f32[pl.ds(p * rows, rows), :]
+    x_bf[...] = x_f32[...].astype(jnp.bfloat16)
+
+    def part_copy(c):
+        return pltpu.make_async_remote_copy(
+            src_ref=part.at[c, gz_other], dst_ref=part_in.at[c], send_sem=part_send.at[c],
+            recv_sem=part_recv.at[c], device_id=(group, gx, gy, gz_other), device_id_type=MESH,
+        )
+
+    def hid_block(c, y, z):
+        return (y * chunks + c) * 2 + z
+
+    def hid_copy(block, send, target):
+        cols = hid.at[:, pl.ds(pl.multiple_of(block * half, half), half)]
+        return pltpu.make_async_remote_copy(
+            src_ref=cols, dst_ref=cols, send_sem=hid_send.at[send],
+            recv_sem=hid_recv.at[block], device_id=target, device_id_type=MESH,
+        )
+
+    hid_targets = (
+        (group, gx, gy_other, gz), (group, gx, gy_other, gz_other), (group, gx, gy, gz_other),
+    )
+
+    def finish(c):
+        part_copy(c).wait_recv()
+        gate = part[c, gz, pl.ds(0, total_rows), :].astype(jnp.float32) + part_in[c, pl.ds(0, total_rows), :].astype(jnp.float32)
+        up = part[c, gz, pl.ds(total_rows, total_rows), :].astype(jnp.float32) + part_in[c, pl.ds(total_rows, total_rows), :].astype(jnp.float32)
+        block = hid_block(c, gy, gz)
+        hid[:, pl.ds(pl.multiple_of(block * half, half), half)] = (jax.nn.silu(gate) * up).astype(jnp.bfloat16)
+        for n, target in enumerate(hid_targets):
+            hid_copy(block, c * 3 + n, target).start()
+
+    @pl.loop(0, chunks)
+    def _(c):
+        weight_copy(gate_ref, gate_buf, gate_sem, c, WIDE).wait()
+        weight_copy(up_ref, up_buf, up_sem, c, WIDE).wait()
+        x = x_bf[...]
+        for n, weight in enumerate((gate_buf, up_buf)):
+            product = jnp.dot(x, weight[c], preferred_element_type=jnp.float32).astype(jnp.bfloat16)
+            for z in range(2):
+                part[c, z, pl.ds(n * total_rows, total_rows), :] = product[:, z * half:(z + 1) * half]
+        part_copy(c).start()
+
+        @pl.when(c > 0)
+        def _():
+            finish(c - 1)
+
+    finish(chunks - 1)
+
+    @pl.loop(0, chunks)
+    def _(c):
+        hid_copy(hid_block(c, gy, gz_other), 0, x_peer).wait_recv()
+        hid_copy(hid_block(c, gy_other, gz), 0, x_peer).wait_recv()
+        hid_copy(hid_block(c, gy_other, gz_other), 0, x_peer).wait_recv()
+
+    def term_copy(n, step):
+        to = lax.rem(gx + step, nx)
+        return pltpu.make_async_remote_copy(
+            src_ref=term.at[n, to], dst_ref=term_in.at[n, gx], send_sem=term_send.at[n, step],
+            recv_sem=term_recv.at[n, gx], device_id=(group, to, gy, gz), device_id_type=MESH,
+        )
+
+    def term_arrival(n, step):
+        sender = lax.rem(gx + nx - step, nx)
+        return sender, pltpu.make_async_remote_copy(
+            src_ref=term.at[n, sender], dst_ref=term_in.at[n, sender], send_sem=term_send.at[n, step],
+            recv_sem=term_recv.at[n, sender], device_id=(group, sender, gy, gz), device_id_type=MESH,
+        )
+
+    @pl.loop(0, out_chunks)
+    def _(n):
+        weight_copy(down_ref, down_buf, down_sem, n, OUT_WIDE).wait()
+        product = jnp.dot(hid[...], down_buf[n], preferred_element_type=jnp.float32)
+        for to in range(nx):
+            block = product[to * out_rows:(to + 1) * out_rows, :]
+            term[n, to] = jnp.concatenate([block[:, :out_half], block[:, out_half:]], axis=0).astype(jnp.bfloat16)
+
+        @pl.loop(1, nx)
+        def _(step):
+            term_copy(n, step).start()
+
+    values = jnp.zeros((out_rows, 1), jnp.float32)
+    for n in range(out_chunks):
+        summed = term[n, gx].astype(jnp.float32)
+        for step in range(1, nx):
+            sender, arrival = term_arrival(n, step)
+            arrival.wait_recv()
+            summed = summed + term_in[n, sender].astype(jnp.float32)
+        for h in range(2):
+            cols = pl.ds(n * OUT_WIDE + h * out_half, out_half)
+            mixed = summed[h * out_rows:(h + 1) * out_rows, :].astype(jnp.bfloat16)
+            out_ref[:, cols] = mixed
+            values = values + jnp.sum(mixed.astype(jnp.float32) * reward_ref[:, cols], axis=1, keepdims=True)
+
+    spread = jnp.concatenate([jnp.where(gx == j, values, jnp.zeros_like(values)) for j in range(nx)], axis=0)
+    spread = jnp.broadcast_to(spread, (total_rows, 128))
+    matches = (ids_ref[...] == lax.broadcasted_iota(jnp.int32, (CANDS, total_rows), 0)).astype(jnp.float32)
+    score_buf[own] = jnp.dot(matches, spread, preferred_element_type=jnp.float32, precision=lax.Precision.HIGHEST)
+
+    def score_copy(slot, step):
+        return pltpu.make_async_remote_copy(
+            src_ref=score_buf.at[slot], dst_ref=score_buf.at[slot], send_sem=score_send.at[step],
+            recv_sem=score_recv.at[slot], device_id=peer(step), device_id_type=MESH,
+        )
+
+    @pl.loop(1, devices)
+    def _(step):
+        score_copy(own, step).start()
+
+    @pl.loop(0, nx)
+    def _(step):
+        tok_copy(mine, step, x_peer).wait_send()
+
+    @pl.loop(1, nx)
+    def _(step):
+        tok_copy(mine, nx + step, x_peer).wait_send()
+
+    @pl.loop(0, chunks)
+    def _(c):
+        part_copy(c).wait_send()
+        for n in range(3):
+            hid_copy(hid_block(c, gy, gz), c * 3 + n, hid_targets[n]).wait_send()
+
+    @pl.loop(0, out_chunks)
+    def _(n):
+        @pl.loop(1, nx)
+        def _(step):
+            term_copy(n, step).wait_send()
+
+    @pl.loop(1, devices)
+    def _(step):
+        score_copy(lax.rem(own + step, devices), step).wait_recv()
+
+    total = score_buf[0]
+    for slot in range(1, devices):
+        total = total + score_buf[slot]
+    score_ref[...] = total
+
+    @pl.loop(1, devices)
+    def _(step):
+        score_copy(own, step).wait_send()
+
+
+def fused_local(nx, tokens, gate_weight, up_weight, down_weight, reward_weight, candidate_ids):
+    rows, width = tokens.shape
+    units = gate_weight.shape[1]
+    depth, out_width = down_weight.shape
+    total_rows = rows * nx * 2
+    pieces = 4
+    chunks, out_chunks = units // WIDE, out_width // OUT_WIDE
+    devices = nx * 4
+    following = jnp.concatenate([candidate_ids[1:], jnp.full((1,), -1, jnp.int32)])
+    last_ids = jnp.where(candidate_ids != following, candidate_ids, -1).reshape(1, total_rows)
+    reward = reward_weight.astype(jnp.float32).reshape(1, out_width)
+    vmem, hbm = pl.BlockSpec(memory_space=pltpu.VMEM), pl.BlockSpec(memory_space=pl.ANY)
+    bf, f32, dma = jnp.bfloat16, jnp.float32, pltpu.SemaphoreType.DMA
+    term_shape = (out_chunks, nx, 4 * rows, OUT_WIDE // 2)
+    mixed, scores = pl.pallas_call(
+        lambda *refs: fused_kernel((nx, rows, pieces, chunks, out_chunks), *refs),
+        out_shape=(
+            jax.ShapeDtypeStruct((2 * rows, out_width), bf),
+            jax.ShapeDtypeStruct((CANDS, 128), f32),
+        ),
+        in_specs=[vmem, hbm, hbm, hbm, vmem, vmem],
+        out_specs=(vmem, vmem),
+        scratch_shapes=[
+            pltpu.VMEM((rows * pieces, width // pieces), f32),
+            pltpu.VMEM((total_rows, width), f32),
+            pltpu.VMEM((total_rows, width), bf),
+            pltpu.VMEM((nx * 2, rows * pieces, width // pieces), bf),
+            pltpu.VMEM((chunks, width, WIDE), bf),
+            pltpu.VMEM((chunks, width, WIDE), bf),
+            pltpu.VMEM((out_chunks, depth, OUT_WIDE), bf),
+            pltpu.VMEM((chunks, 2, 2 * total_rows, WIDE // 2), bf),
+            pltpu.VMEM((chunks, 2 * total_rows, WIDE // 2), bf),
+            pltpu.VMEM((total_rows, depth), bf),
+            pltpu.VMEM(term_shape, bf),
+            pltpu.VMEM(term_shape, bf),
+            pltpu.VMEM((devices, CANDS, 128), f32),
+            dma((chunks,)), dma((chunks,)), dma((out_chunks,)),
+            dma((nx * 2,)), dma((nx * 2,)),
+            dma((chunks,)), dma((chunks,)),
+            dma((chunks * 3,)), dma((chunks * 4,)),
+            dma((out_chunks, nx)), dma((out_chunks, nx)),
+            dma((devices,)), dma((devices,)),
+        ],
+        compiler_params=pltpu.CompilerParams(
+            collective_id=0, has_side_effects=True, vmem_limit_bytes=VMEM_BYTES
+        ),
+        cost_estimate=pl.CostEstimate(
+            flops=2 * total_rows * (2 * width * units + depth * out_width),
+            bytes_accessed=2 * (2 * width * units + depth * out_width), transcendentals=0,
+        ),
+    )(tokens, gate_weight, up_weight, down_weight, reward, last_ids)
+    return mixed, scores[:, 0]
+
+
+def fits_fused(mesh, tokens, gate_weight, down_weight):
+    nx, ny, nz = mesh.shape["gx"], mesh.shape["gy"], mesh.shape["gz"]
+    if ny != 2 or nz != 2:
+        return False
+    rows, units = tokens.shape[0] // (mesh.shape["groups"] * nx * ny), gate_weight.shape[1] // (nx * ny)
+    out_width = down_weight.shape[1] // (ny * nz)
+    weights = 2 * (2 * units * gate_weight.shape[0] // nz + ny * units * out_width)
+    return (
+        rows % 4 == 0 and (rows * 2 * nx) % 16 == 0 and units % WIDE == 0 and out_width % OUT_WIDE == 0
+        and weights < 48 * 1024 * 1024 and rows * nx * ny <= 128
+    )
+
+
 def solution(mesh):
+    def call(tokens, gate_weight, up_weight, down_weight, reward_weight, candidate_ids):
+        fused = fits_fused(mesh, tokens, gate_weight, down_weight)
+        local = (lambda *blocks: fused_local(mesh.shape["gx"], *blocks)) if fused else plain_local
+        return placed_call(mesh, local)(
+            tokens, gate_weight, up_weight, down_weight, reward_weight, candidate_ids
+        )
+
+    return call
+
+
+def placed_call(mesh, local):
     placed = (
         P(("groups", "gx", "gy"), "gz"),
         P("gz", ("gx", "gy")),

time: 157 us -> 57.4 us (0.37)
  blocking collectives: 75.8 us -> 0 us
  Pallas kernels: 0 us -> 50.4 us
  waiting for transfers between devices: 41.7 us -> 0 us
  matrix products: 20.8 us -> 0 us
  between operations: 14.1 us -> 0.64 us
  other arithmetic: 0.47 us -> 2.52 us
    pallas_call x0 -> x1, Pallas kernels: none -> 50.4 us  [fused_local(): pl.pallas_call(lambda *refs: fused_kernel((nx, rows, pieces, chunks, out_...]
    all_gather x2 -> x0, blocking collectives: 45.8 us -> none  [the longest x1 34.9 us: local(): all_tokens = lax.all_gather(tokens, ('gx', 'gy'), axis=0, tiled=True)]
    psum x1 -> x0, blocking collectives: 30 us -> none  [local(): scores = lax.psum(partial_scores, ('gx', 'gy', 'gz'))]
    reduce_scatter x1 -> x0, waiting for transfers between devices: 21.7 us -> none  [local(): lax.psum_scatter(jnp.dot(hidden_all, down_weight, preferred_element_type=...]
    dot_general x3 -> x0, matrix products: 20.8 us -> none  [the longest x1 11.3 us: local(): jnp.dot(all_tokens, paired, preferred_element_type=jnp.float32)]
    psum x1 -> x0, waiting for transfers between devices: 19.9 us -> none  [combine_pairs(): lax.psum(partial_value.astype(jnp.bfloat16), 'gz').astype(jnp.float32)]
    reshape x0 -> x2, other arithmetic: none -> 2.52 us  [the longest x1 1.29 us: fused_local(): reward = reward_weight.astype(jnp.float32).reshape(1, out_width)]
  transfers between devices with their start and end apart: 2 -> 0, of which waited for: 2 -> 0; matrix products, arithmetic and copies ran while one was open for 0% -> 0% of each run, Pallas kernels for 0% -> 0%
where the time goes in v1:
time: 57.4 us; the launch traced here: 57.1 us
  Pallas kernels  50.4 us (88%)
  local copies, waits for them, and re-layouts  3.59 us (6%)
  other arithmetic  2.52 us (4%)
  between operations  0.64 us (1%)
    pallas_call x1, Pallas kernels, fused_local(): pl.pallas_call(lambda *refs: fused_kernel((nx, rows, pieces, chunks, out_...  50.4 us
    unnamed x1, local copies, waits for them, and re-layouts  1.54 us
    slice x1, local copies, waits for them, and re-layouts, fused_local(): return (mixed, scores[:, 0])  1.32 us
    reshape x1, other arithmetic, fused_local(): reward = reward_weight.astype(jnp.float32).reshape(1, out_width)  1.29 us
    reshape x1, other arithmetic, fused_local(): jnp.where(candidate_ids != following, candidate_ids, -1)  1.24 us

profile of v1, /device:TPU:0, one launch (start us, length us, event | category | flops | bytes accessed | tf_op | source)
XLA Modules:
  0.0 57.1 jit_solution(17287624279219717558)
XLA Ops:
  0.6 0.7 %slice.6 = s32[95]{0:T(128)S(1)} slice(s32[96]{0:T(128)} %param.11), slice={[1:96]} | slice | bytes 760 | tf_op jit(solution)/shard_map/slice | solution.py:286
  1.4 1.2 %fusion.refs_5_ = s32[1,96]{1,0:T(1,128)} fusion(s32[96]{0:T(128)} %param.11, s32[1]{0:T(128)} %constant.0.clone.1, s32[95]{0:T(128)S(1)} %slice.6), kind=kLoop, calls=%fused_computation.2 | loop fusion | flops 288 | bytes 1152 | tf_op jit(solution)/shard_map/reshape | solution.py:287
  2.6 1.3 %reshape.15 = f32[2048]{0:T(1024)} convert(bf16[2048]{0:T(1024)(128)(2,1)} %param.10) | non-fusion elementwise | flops 2048 | bytes 12288 | tf_op jit(solution)/shard_map/reshape | solution.py:288
  3.9 50.4 %shard_map.77 = (bf16[24,2048]{1,0:T(8,128)(2,1)}, f32[16,128]{1,0:T(8,128)}) custom-call(bf16[12,4096]{1,0:T(8,128)(2,1)} %refs_0_.1, bf16[4096,1792]{1,0:T(8,128)(2,1)} %refs_1_.1, bf16[4096,1792]{1,0:T(8,128)(2,1)} %refs_2_.1, bf16[3584,2048]{1,0:T(8,128)(2,1)} %refs_3_.1, f32[1,2048]{1,0:T(1,128)} %bitcast.3, s32[1,96]{1,0:T(1,128)} %fusion.refs_5_), custom_call_target="tpu_custom_call" | custom-call | flops 4227858432 | bytes 44040192 | tf_op jit(solution)/shard_map/pallas_call | solution.py:292
  54.3 1.3 %slice_reduce_fusion = f32[16]{0:T(128)} fusion(f32[16,128]{1,0:T(8,128)} %get-tuple-element.5), kind=kLoop, calls=%fused_computation | loop fusion | bytes 128 | tf_op jit(solution)/shard_map/slice | solution.py:329
  55.6 1.5 %copy.9 = bf16[24,2048]{1,0:T(8,128)(2,1)} copy(bf16[24,2048]{1,0:T(8,128)(2,1)} %get-tuple-element.8) | data formatting | bytes 196608

commit v2 on v0

--- a/solution.py
+++ b/solution.py
@@ -1,6 +1,8 @@
 import jax
 import jax.numpy as jnp
 from jax import lax
+from jax.experimental import pallas as pl
+from jax.experimental.pallas import tpu as pltpu
 from jax.sharding import PartitionSpec as P
 
 CANDS = 16
@@ -19,7 +21,7 @@
     return swiglu_pair(summed, unit_count)
 
 
-def local(tokens, gate_weight, up_weight, down_weight, reward_weight, candidate_ids):
+def plain_local(tokens, gate_weight, up_weight, down_weight, reward_weight, candidate_ids):
     unit_count = gate_weight.shape[1]
     paired = jnp.concatenate([gate_weight, up_weight], axis=1)
     local_rows = tokens.shape[0]
@@ -50,7 +52,357 @@
     return (summed_out, scores)
 
 
+MESH = pl.DeviceIdType.MESH
+WIDE = 256
+OUT_WIDE = 512
+PIECES = 2
+GROUP = 2
+SUBS = 4
+VMEM_BYTES = 60 * 1024 * 1024
+
+
+def fused_kernel(
+    sizes, tok_ref, gate_ref, up_ref, down_ref, reward_ref, ids_ref, out_ref, score_ref,
+    tok_f32, x_f32, x_bf, blocks, gate_buf, up_buf, down_buf, part, part_in, hid, term, term_in, score_buf, sums,
+    gate_sem, up_sem, down_sem, tok_send, tok_recv, part_send, part_recv, hid_send, hid_recv,
+    term_send, term_recv, score_send, score_recv,
+):
+    nx, rows, pieces, chunks, out_chunks = sizes
+    cut = tok_ref.shape[1] // pieces
+    sub = cut // SUBS
+    out_rows = 2 * rows
+    total_rows = x_bf.shape[0]
+    half = WIDE // 2
+    out_half = OUT_WIDE // 2
+    group, gx, gy, gz = (lax.axis_index(a) for a in ("groups", "gx", "gy", "gz"))
+    gy_other, gz_other = 1 - gy, 1 - gz
+    z_peers = [(group, lax.rem(gx + step, nx), gy, gz) for step in range(1, nx)]
+    near_peers = [(group, gx, gy_other, gz), (group, gx, gy_other, gz_other), (group, gx, gy, gz_other)]
+    near_slots = [gy_other * 2 + gz, gy_other * 2 + gz_other, gy * 2 + gz_other]
+    own = gy * 2 + gz
+
+    def row_copy(source, target, sem, p):
+        return pltpu.make_async_copy(source.at[pl.ds(pl.multiple_of(p * cut, cut), cut)], target.at[p], sem.at[p])
+
+    def down_copy(n):
+        cols = pl.ds(pl.multiple_of(n * OUT_WIDE, OUT_WIDE), OUT_WIDE)
+        return pltpu.make_async_copy(down_ref.at[:, cols], down_buf.at[n], down_sem.at[n])
+
+    @pl.loop(0, pieces)
+    def _(p):
+        row_copy(gate_ref, gate_buf, gate_sem, p).start()
+        row_copy(up_ref, up_buf, up_sem, p).start()
+
+    @pl.loop(0, out_chunks)
+    def _(n):
+        down_copy(n).start()
+
+    barrier = pltpu.get_barrier_semaphore()
+
+    for target in z_peers + near_peers:
+        pl.semaphore_signal(barrier, inc=1, device_id=target, device_id_type=MESH)
+
+    mine = gx * 2 + gy
+    for p in range(pieces):
+        for q in range(SUBS):
+            tok_f32[p, pl.ds(q * rows, rows), :] = tok_ref[:, pl.ds(p * cut + q * sub, sub)].astype(jnp.float32)
+        blocks[p, mine] = tok_f32[p].astype(jnp.bfloat16)
+    pl.semaphore_wait(barrier, nx + 2)
+
+    def tok_copy(p, slot, send, target):
+        return pltpu.make_async_remote_copy(
+            src_ref=blocks.at[p, slot], dst_ref=blocks.at[p, slot], send_sem=tok_send.at[p, send],
+            recv_sem=tok_recv.at[p, slot], device_id=target, device_id_type=MESH,
+        )
+
+    x_peer = (group, gx, gy_other, gz)
+
+    @pl.loop(0, pieces)
+    def _(p):
+        tok_copy(p, mine, 0, x_peer).start()
+
+        @pl.loop(1, nx)
+        def _(step):
+            tok_copy(p, mine, step, (group, lax.rem(gx + step, nx), gy, gz)).start()
+
+    def forward(p):
+        @pl.loop(1, nx)
+        def _(step):
+            slot = lax.rem(gx + nx - step, nx) * 2 + gy
+            tok_copy(p, slot, 0, x_peer).wait_recv()
+            tok_copy(p, slot, nx + step, x_peer).start()
+
+    spans = [(c, min(c + GROUP, chunks)) for c in range(0, chunks, GROUP)]
+    half_units = chunks * half
+    core_peer = (group, gx, gy, gz_other)
+    across = gy_other * 2 + gz
+
+    def part_copy(g):
+        first, end = spans[g]
+        return pltpu.make_async_remote_copy(
+            src_ref=part.at[gz_other, pl.ds(first, end - first)], dst_ref=part_in.at[pl.ds(first, end - first)],
+            send_sem=part_send.at[g], recv_sem=part_recv.at[g],
+            device_id=(group, gx, gy, gz_other), device_id_type=MESH,
+        )
+
+    def hid_copy(g, slot, send, target):
+        first, end = spans[g]
+        cols = hid.at[:, pl.ds(pl.multiple_of(slot * half_units + first * half, half), (end - first) * half)]
+        return pltpu.make_async_remote_copy(
+            src_ref=cols, dst_ref=cols, send_sem=hid_send.at[g, send],
+            recv_sem=hid_recv.at[g, slot], device_id=target, device_id_type=MESH,
+        )
+
+    def finish(g):
+        part_copy(g).wait_recv()
+
+        @pl.loop(*spans[g])
+        def _(c):
+            gate, up = (
+                part[gz, c, pl.ds(n * total_rows, total_rows), :].astype(jnp.float32)
+                + part_in[c, pl.ds(n * total_rows, total_rows), :].astype(jnp.float32)
+                for n in range(2)
+            )
+            cols = pl.ds(pl.multiple_of(own * half_units + c * half, half), half)
+            hid[:, cols] = (jax.nn.silu(gate) * up).astype(jnp.bfloat16)
+
+        hid_copy(g, own, 0, x_peer).start()
+        hid_copy(g, own, 1, core_peer).start()
+
+    forward(0)
+    for p in range(pieces):
+        if p + 1 < pieces:
+            forward(p + 1)
+
+        @pl.loop(0, nx)
+        def _(step):
+            slot = lax.rem(gx + nx - step, nx) * 2 + gy_other
+            tok_copy(p, slot, 0, x_peer).wait_recv()
+
+        for d in range(nx * 2):
+            tok_f32[p] = blocks[p, d].astype(jnp.float32)
+            for q in range(SUBS):
+                x_f32[pl.ds(d * rows, rows), pl.ds(q * sub, sub)] = tok_f32[p, pl.ds(q * rows, rows), :]
+        x_bf[...] = x_f32[...].astype(jnp.bfloat16)
+        row_copy(gate_ref, gate_buf, gate_sem, p).wait()
+        row_copy(up_ref, up_buf, up_sem, p).wait()
+
+        def multiply(start, end):
+            @pl.loop(start, end)
+            def _(c):
+                x = x_bf[...]
+                low = pl.ds(pl.multiple_of(c * half, half), half)
+                high = pl.ds(pl.multiple_of(half_units + c * half, half), half)
+                for n, weight in enumerate((gate_buf, up_buf)):
+                    both = jnp.concatenate([weight[p, :, low], weight[p, :, high]], axis=1)
+                    product = jnp.dot(x, both, preferred_element_type=jnp.float32)
+                    if p > 0:
+                        product = product + sums[c, n]
+                    if p + 1 < pieces:
+                        sums[c, n] = product
+                    else:
+                        product = product.astype(jnp.bfloat16)
+                        for z in range(2):
+                            part[z, c, pl.ds(n * total_rows, total_rows), :] = product[:, z * half:(z + 1) * half]
+
+        if p + 1 < pieces:
+            multiply(0, chunks)
+        else:
+            for g, span in enumerate(spans):
+                multiply(*span)
+                part_copy(g).start()
+                if g > 0:
+                    finish(g - 1)
+
+    finish(len(spans) - 1)
+    for g in range(len(spans)):
+        hid_copy(g, across, 0, x_peer).wait_recv()
+        hid_copy(g, across, 2, core_peer).start()
+    for g in range(len(spans)):
+        hid_copy(g, gy * 2 + gz_other, 1, core_peer).wait_recv()
+        hid_copy(g, gy_other * 2 + gz_other, 2, core_peer).wait_recv()
+
+    def term_copy(n, step):
+        to = lax.rem(gx + step, nx)
+        return pltpu.make_async_remote_copy(
+            src_ref=term.at[n, to], dst_ref=term_in.at[n, gx], send_sem=term_send.at[n, step],
+            recv_sem=term_recv.at[n, gx], device_id=(group, to, gy, gz), device_id_type=MESH,
+        )
+
+    def term_arrival(n, step):
+        sender = lax.rem(gx + nx - step, nx)
+        return sender, pltpu.make_async_remote_copy(
+            src_ref=term.at[n, sender], dst_ref=term_in.at[n, sender], send_sem=term_send.at[n, step],
+            recv_sem=term_recv.at[n, sender], device_id=(group, sender, gy, gz), device_id_type=MESH,
+        )
+
+    @pl.loop(0, out_chunks)
+    def _(n):
+        down_copy(n).wait()
+        product = jnp.dot(hid[...], down_buf[n], preferred_element_type=jnp.float32)
+        for to in range(nx):
+            block = product[to * out_rows:(to + 1) * out_rows, :]
+            term[n, to] = jnp.concatenate([block[:, :out_half], block[:, out_half:]], axis=0).astype(jnp.bfloat16)
+
+        @pl.loop(1, nx)
+        def _(step):
+            term_copy(n, step).start()
+
+    values = jnp.zeros((out_rows, 1), jnp.float32)
+    reward = reward_ref[...].astype(jnp.float32)
+    for n in range(out_chunks):
+        summed = term[n, gx].astype(jnp.float32)
+        for step in range(1, nx):
+            sender, arrival = term_arrival(n, step)
+            arrival.wait_recv()
+            summed = summed + term_in[n, sender].astype(jnp.float32)
+        for h in range(2):
+            cols = pl.ds(n * OUT_WIDE + h * out_half, out_half)
+            mixed = summed[h * out_rows:(h + 1) * out_rows, :].astype(jnp.bfloat16)
+            out_ref[:, cols] = mixed
+            for q in range(out_half // 128):
+                line = (n * OUT_WIDE + h * out_half) // 128 + q
+                scaled = mixed[:, q * 128:(q + 1) * 128].astype(jnp.float32) * reward[line:line + 1, :]
+                values = values + jnp.sum(scaled, axis=1, keepdims=True)
+
+    spread = jnp.concatenate([jnp.where(gx == j, values, jnp.zeros_like(values)) for j in range(nx)], axis=0)
+    spread = jnp.broadcast_to(spread, (total_rows, 128))
+    place = lax.broadcasted_iota(jnp.int32, (CANDS, total_rows), 1)
+    same = ids_ref[...] == lax.broadcasted_iota(jnp.int32, (CANDS, total_rows), 0)
+    last = jnp.max(jnp.where(same, place, -1), axis=1, keepdims=True)
+    matches = (place == last).astype(jnp.float32)
+    score_buf[own] = jnp.dot(matches, spread, preferred_element_type=jnp.float32, precision=lax.Precision.HIGHEST)
+
+    def score_copy(slot, send, target):
+        return pltpu.make_async_remote_copy(
+            src_ref=score_buf.at[slot], dst_ref=score_buf.at[slot], send_sem=score_send.at[send],
+            recv_sem=score_recv.at[slot], device_id=target, device_id_type=MESH,
+        )
+
+    for n, target in enumerate(near_peers):
+        score_copy(own, n, target).start()
+
+    for slot, target in zip(near_slots, near_peers):
+        score_copy(slot, 0, target).wait_recv()
+    score_buf[4 + gx] = (score_buf[0] + score_buf[1]) + (score_buf[2] + score_buf[3])
+    for n, target in enumerate(z_peers):
+        score_copy(4 + gx, 3 + n, target).start()
+    for step in range(1, nx):
+        score_copy(4 + lax.rem(gx + step, nx), 0, z_peers[step - 1]).wait_recv()
+    total = score_buf[4]
+    for j in range(1, nx):
+        total = total + score_buf[4 + j]
+    diagonal = lax.broadcasted_iota(jnp.int32, (CANDS, 128), 0) == lax.broadcasted_iota(jnp.int32, (CANDS, 128), 1)
+    score_ref[...] = jnp.sum(jnp.where(diagonal, total, 0.0), axis=0, keepdims=True)[:, :CANDS]
+
+
+    @pl.loop(0, pieces)
+    def _(p):
+        @pl.loop(0, nx)
+        def _(step):
+            tok_copy(p, mine, step, x_peer).wait_send()
+
+        @pl.loop(1, nx)
+        def _(step):
+            tok_copy(p, mine, nx + step, x_peer).wait_send()
+
+    for g in range(len(spans)):
+        part_copy(g).wait_send()
+        hid_copy(g, own, 0, x_peer).wait_send()
+        hid_copy(g, own, 1, core_peer).wait_send()
+        hid_copy(g, across, 2, core_peer).wait_send()
+
+    @pl.loop(0, out_chunks)
+    def _(n):
+        @pl.loop(1, nx)
+        def _(step):
+            term_copy(n, step).wait_send()
+
+    for n, target in enumerate(near_peers):
+        score_copy(own, n, target).wait_send()
+    for n, target in enumerate(z_peers):
+        score_copy(4 + gx, 3 + n, target).wait_send()
+
+
+def fused_local(nx, tokens, gate_weight, up_weight, down_weight, reward_weight, candidate_ids):
+    rows, width = tokens.shape
+    units = gate_weight.shape[1]
+    depth, out_width = down_weight.shape
+    total_rows = rows * nx * 2
+    pieces, cut = PIECES, width // PIECES
+    chunks, out_chunks = units // WIDE, out_width // OUT_WIDE
+    groups = pl.cdiv(chunks, GROUP)
+    ids = candidate_ids.reshape(1, total_rows)
+    reward = reward_weight.reshape(out_width // 128, 128)
+    vmem, hbm = pl.BlockSpec(memory_space=pltpu.VMEM), pl.BlockSpec(memory_space=pl.ANY)
+    bf, f32, dma = jnp.bfloat16, jnp.float32, pltpu.SemaphoreType.DMA
+    term_shape = (out_chunks, nx, 4 * rows, OUT_WIDE // 2)
+    mixed, scores = pl.pallas_call(
+        lambda *refs: fused_kernel((nx, rows, pieces, chunks, out_chunks), *refs),
+        out_shape=(
+            jax.ShapeDtypeStruct((2 * rows, out_width), bf),
+            jax.ShapeDtypeStruct((1, CANDS), f32),
+        ),
+        in_specs=[vmem, hbm, hbm, hbm, vmem, vmem],
+        out_specs=(vmem, vmem),
+        scratch_shapes=[
+            pltpu.VMEM((pieces, rows * SUBS, cut // SUBS), f32),
+            pltpu.VMEM((total_rows, cut), f32),
+            pltpu.VMEM((total_rows, cut), bf),
+            pltpu.VMEM((pieces, nx * 2, rows * SUBS, cut // SUBS), bf),
+            pltpu.VMEM((pieces, cut, units), bf),
+            pltpu.VMEM((pieces, cut, units), bf),
+            pltpu.VMEM((out_chunks, depth, OUT_WIDE), bf),
+            pltpu.VMEM((2, chunks, 2 * total_rows, WIDE // 2), bf),
+            pltpu.VMEM((chunks, 2 * total_rows, WIDE // 2), bf),
+            pltpu.VMEM((total_rows, depth), bf),
+            pltpu.VMEM(term_shape, bf),
+            pltpu.VMEM(term_shape, bf),
+            pltpu.VMEM((4 + nx, CANDS, 128), f32),
+            pltpu.VMEM((chunks, 2, total_rows, WIDE), f32),
+            dma((pieces,)), dma((pieces,)), dma((out_chunks,)),
+            dma((pieces, nx * 2)), dma((pieces, nx * 2)),
+            dma((groups,)), dma((groups,)),
+            dma((groups, 3)), dma((groups, 4)),
+            dma((out_chunks, nx)), dma((out_chunks, nx)),
+            dma((4 + nx,)), dma((4 + nx,)),
+        ],
+        compiler_params=pltpu.CompilerParams(
+            collective_id=0, has_side_effects=True, vmem_limit_bytes=VMEM_BYTES
+        ),
+        cost_estimate=pl.CostEstimate(
+            flops=2 * total_rows * (2 * width * units + depth * out_width),
+            bytes_accessed=2 * (2 * width * units + depth * out_width), transcendentals=0,
+        ),
+    )(tokens, gate_weight, up_weight, down_weight, reward, ids)
+    return mixed, scores.reshape(CANDS)
+
+
+def fits_fused(mesh, tokens, gate_weight, down_weight):
+    nx, ny, nz = mesh.shape["gx"], mesh.shape["gy"], mesh.shape["gz"]
+    if ny != 2 or nz != 2:
+        return False
+    rows, units = tokens.shape[0] // (mesh.shape["groups"] * nx * ny), gate_weight.shape[1] // (nx * ny)
+    out_width = down_weight.shape[1] // (ny * nz)
+    weights = 2 * (2 * units * gate_weight.shape[0] // nz + ny * units * out_width)
+    return (
+        rows % 4 == 0 and gate_weight.shape[0] % (2048 * nz) == 0 and (rows * 2 * nx) % 16 == 0 and units % WIDE == 0 and out_width % OUT_WIDE == 0
+        and weights < 48 * 1024 * 1024 and rows * nx * ny <= 128
+    )
+
+
 def solution(mesh):
+    def call(tokens, gate_weight, up_weight, down_weight, reward_weight, candidate_ids):
+        fused = fits_fused(mesh, tokens, gate_weight, down_weight)
+        local = (lambda *blocks: fused_local(mesh.shape["gx"], *blocks)) if fused else plain_local
+        return placed_call(mesh, local)(
+            tokens, gate_weight, up_weight, down_weight, reward_weight, candidate_ids
+        )
+
+    return call
+
+
+def placed_call(mesh, local):
     placed = (
         P(("groups", "gx", "gy"), "gz"),
         P("gz", ("gx", "gy")),

time: 157 us -> 53.6 us (0.34)
  blocking collectives: 75.8 us -> 0 us
  Pallas kernels: 0 us -> 50.1 us
  waiting for transfers between devices: 41.7 us -> 0 us
  matrix products: 20.8 us -> 0 us
  between operations: 14.1 us -> 0.64 us
    pallas_call x0 -> x1, Pallas kernels: none -> 50.1 us  [fused_local(): pl.pallas_call(lambda *refs: fused_kernel((nx, rows, pieces, chunks, out_...]
    all_gather x2 -> x0, blocking collectives: 45.8 us -> none  [the longest x1 34.9 us: local(): all_tokens = lax.all_gather(tokens, ('gx', 'gy'), axis=0, tiled=True)]
    psum x1 -> x0, blocking collectives: 30 us -> none  [local(): scores = lax.psum(partial_scores, ('gx', 'gy', 'gz'))]
    reduce_scatter x1 -> x0, waiting for transfers between devices: 21.7 us -> none  [local(): lax.psum_scatter(jnp.dot(hidden_all, down_weight, preferred_element_type=...]
    dot_general x3 -> x0, matrix products: 20.8 us -> none  [the longest x1 11.3 us: local(): jnp.dot(all_tokens, paired, preferred_element_type=jnp.float32)]
    psum x1 -> x0, waiting for transfers between devices: 19.9 us -> none  [combine_pairs(): lax.psum(partial_value.astype(jnp.bfloat16), 'gz').astype(jnp.float32)]
    unnamed x6 -> x2, local copies, waits for them, and re-layouts: 0.19 us -> 2.73 us
    slice x1 -> x0, local copies, waits for them, and re-layouts: 2.49 us -> none  [swiglu_pair(): gate_part = split_pair[:, :, 0, :].reshape(row_count, -1)]
  transfers between devices with their start and end apart: 2 -> 0, of which waited for: 2 -> 0; matrix products, arithmetic and copies ran while one was open for 0% -> 0% of each run, Pallas kernels for 0% -> 0%
where the time goes in v2:
time: 53.6 us; the launch traced here: 53.4 us
  Pallas kernels  50.1 us (93%)
  local copies, waits for them, and re-layouts  2.73 us (5%)
  between operations  0.64 us (1%)
    pallas_call x1, Pallas kernels, fused_local(): pl.pallas_call(lambda *refs: fused_kernel((nx, rows, pieces, chunks, out_...  50.1 us
    unnamed x2, local copies, waits for them, and re-layouts  2.73 us

profile of v2, /device:TPU:0, one launch (start us, length us, event | category | flops | bytes accessed | tf_op | source)
XLA Modules:
  0.0 53.4 jit_solution(8369640802399024536)
XLA Ops:
  0.6 50.1 %shard_map.77 = (bf16[24,2048]{1,0:T(8,128)(2,1)}, f32[1,16]{1,0:T(1,128)}) custom-call(bf16[12,4096]{1,0:T(8,128)(2,1)} %refs_0_.1, bf16[4096,1792]{1,0:T(8,128)(2,1)} %refs_1_.1, bf16[4096,1792]{1,0:T(8,128)(2,1)} %refs_2_.1, bf16[3584,2048]{1,0:T(8,128)(2,1)} %refs_3_.1, bf16[16,128]{1,0:T(8,128)(2,1)} %bitcast.3, s32[1,96]{1,0:T(1,128)} %bitcast.4), custom_call_target="tpu_custom_call" | custom-call | flops 4227858432 | bytes 44040192 | tf_op jit(solution)/shard_map/pallas_call | solution.py:340
  50.7 1.5 %copy.10 = bf16[24,2048]{1,0:T(8,128)(2,1)} copy(bf16[24,2048]{1,0:T(8,128)(2,1)} %get-tuple-element.8) | data formatting | bytes 196608
  52.3 1.2 %copy.11 = f32[16]{0:T(128)} copy(f32[16]{0:T(128)} %bitcast.5) | data formatting | bytes 128

commit v3 on v2

--- a/solution.py
+++ b/solution.py
@@ -54,7 +54,7 @@
 
 MESH = pl.DeviceIdType.MESH
 WIDE = 256
-OUT_WIDE = 512
+OUT_WIDE = 256
 PIECES = 2
 GROUP = 2
 SUBS = 4

time: 53.6 us -> 53.8 us (level)
  no operation moved by 1% of the time
where the time goes in v3:
time: 53.8 us; the launch traced here: 53.6 us
  Pallas kernels  50.2 us (93%)
  local copies, waits for them, and re-layouts  2.73 us (5%)
  between operations  0.64 us (1%)
    pallas_call x1, Pallas kernels, fused_local(): pl.pallas_call(lambda *refs: fused_kernel((nx, rows, pieces, chunks, out_...  50.2 us
    unnamed x2, local copies, waits for them, and re-layouts  2.73 us

profile of v3, /device:TPU:0, one launch (start us, length us, event | category | flops | bytes accessed | tf_op | source)
XLA Modules:
  0.0 53.6 jit_solution(16850774121901848124)
XLA Ops:
  0.6 50.2 %shard_map.77 = (bf16[24,2048]{1,0:T(8,128)(2,1)}, f32[1,16]{1,0:T(1,128)}) custom-call(bf16[12,4096]{1,0:T(8,128)(2,1)} %refs_0_.1, bf16[4096,1792]{1,0:T(8,128)(2,1)} %refs_1_.1, bf16[4096,1792]{1,0:T(8,128)(2,1)} %refs_2_.1, bf16[3584,2048]{1,0:T(8,128)(2,1)} %refs_3_.1, bf16[16,128]{1,0:T(8,128)(2,1)} %bitcast.3, s32[1,96]{1,0:T(1,128)} %bitcast.4), custom_call_target="tpu_custom_call" | custom-call | flops 4227858432 | bytes 44040192 | tf_op jit(solution)/shard_map/pallas_call | solution.py:340
  50.8 1.5 %copy.10 = bf16[24,2048]{1,0:T(8,128)(2,1)} copy(bf16[24,2048]{1,0:T(8,128)(2,1)} %get-tuple-element.8) | data formatting | bytes 196608
  52.4 1.2 %copy.11 = f32[16]{0:T(128)} copy(f32[16]{0:T(128)} %bitcast.5) | data formatting | bytes 128
